TPU v7x, 32 devices: a whole 2x2x4 slice. The times are simulated.
32 devices in a mesh: band: 2 (over y), strip: 4 (over z), src: 4 (over x, core).
Axes of the slice: x: 2, y: 2, z: 4, core: 2. Of those that a mesh axis runs over, the one named last changes fastest.
Arguments:
- theta: float32 [1024, 512], P(('band', 'strip')), parts along dimension 0, may hold values from -8 to 8
- target: int32 [1024, 512], P(('band', 'strip')), parts along dimension 0, may hold values 0 or 1
- source_shift: int32 [32, 2], P('src'), may hold values from -16 to 16
- source_weight: float32 [32], P('src'), may hold values from 0.14 to 7.1
Outputs:
- theta_final: float32 [1024, 512], P(('band', 'strip')), parts along dimension 0
- resist: float32 [1024, 512], P(('band', 'strip')), parts along dimension 0
There are 2 independent parts, one for each index of `band`. A program takes and returns all parts, laid end to end along the dimension named above; an argument that names none is the same for every part. Nothing has to cross between parts.
All inputs are finite; a program needn't handle non-finite values. No bound on the sum of `target` on one device may be relied on, other than what follows from the above.
Results may differ from a plain program's by a relative error of at most 0.0055.
The roundings to bfloat16 on the way count: a program that leaves them out, or rounds other values in their place, can miss the bound.
Values may be sent and summed in bfloat16 or wider, within the bound.
A program may use at most 64 MiB of HBM per device.

v0:
```python
import math

import jax
import jax.numpy as jnp
from jax import lax
from jax.sharding import PartitionSpec as P

ROWS = 128
COLS = 512
HALO = 64
FREQ = 128
SRC_DEV = 8
ITERS = 2


steepness = 20.0
dose_level = 0.27
step_size = 1.0
epsilon = 1e-06


def extended(cells, sides, width):
    for axis, dim in sides:
        count = lax.axis_size(axis)
        head = lax.slice_in_dim(cells, 0, width, axis=dim)
        tail = lax.slice_in_dim(cells, cells.shape[dim] - width, cells.shape[dim], axis=dim)
        cells = jnp.concatenate(
            [
                lax.ppermute(tail, axis, [(i, (i + 1) % count) for i in range(count)]),
                cells,
                lax.ppermute(head, axis, [((i + 1) % count, i) for i in range(count)]),
            ],
            axis=dim,
        )
    return cells


def shifted(array, axis, by):
    size = lax.axis_size(axis)
    return lax.ppermute(array, axis, [(i, (i + by) % size) for i in range(size)])


def phase_pair(freq_ids, points, period):
    index = freq_ids[:, None] % period * points[None, :] % period
    angle = 2.0 * math.pi / period * index.astype(jnp.float32)
    return (jnp.cos(angle), jnp.sin(angle))


def build_tables():
    freq_ids = jnp.arange(FREQ, dtype=jnp.int32) - FREQ // 2
    win_len = ROWS + 2 * HALO
    row_cos, row_sin = phase_pair(freq_ids, jnp.arange(win_len, dtype=jnp.int32), win_len)
    forward_rows = (jnp.concatenate([row_cos, -row_sin], 0) / win_len).astype(jnp.bfloat16)
    col_cos, col_sin = phase_pair(freq_ids, jnp.arange(COLS, dtype=jnp.int32), COLS)
    real_part = jnp.concatenate([col_cos.T, -col_sin.T], 1) / COLS
    imag_part = jnp.concatenate([col_sin.T, col_cos.T], 1) / COLS
    forward_cols = jnp.stack([real_part, imag_part], 0).astype(jnp.bfloat16)
    inverse_cols = jnp.concatenate(
        [jnp.concatenate([col_cos, col_sin], 1), jnp.concatenate([-col_sin, col_cos], 1)], 0
    ).astype(jnp.bfloat16)
    inner_cos, inner_sin = phase_pair(freq_ids, jnp.arange(ROWS, dtype=jnp.int32) + HALO, win_len)
    inner_cos, inner_sin = (inner_cos.T, inner_sin.T)
    inverse_rows = jnp.stack(
        [jnp.stack([inner_cos, -inner_sin], 1), jnp.stack([inner_sin, inner_cos], 1)], 0
    ).astype(jnp.bfloat16)
    return (forward_rows, forward_cols, inverse_cols, inverse_rows)


def pupil_of(shifts):
    grid = jnp.arange(FREQ, dtype=jnp.int32) - FREQ // 2
    along_k = grid[None, :] + shifts[:, 0:1]
    along_l = grid[None, :] + shifts[:, 1:2]
    radius = FREQ // 4
    inside = (
        along_k[:, :, None] * along_k[:, :, None] + along_l[:, None, :] * along_l[:, None, :]
        <= radius * radius
    )
    pupil = inside.astype(jnp.float32)
    return jnp.concatenate([pupil, pupil], 2).astype(jnp.bfloat16)


def imaging(window, pupil, weights, tables, total_sources):
    forward_rows, forward_cols, inverse_cols, inverse_rows = tables
    count = pupil.shape[0]
    half = jnp.dot(forward_rows, window, preferred_element_type=jnp.float32).astype(jnp.bfloat16)
    spectrum = jnp.einsum(
        "pkc,pcl->kl", half.reshape(2, FREQ, COLS), forward_cols, preferred_element_type=jnp.float32
    ).astype(jnp.bfloat16)
    passed = pupil * spectrum[None]
    columns = jnp.dot(
        passed.reshape(count * FREQ, 2 * FREQ), inverse_cols, preferred_element_type=jnp.float32
    ).astype(jnp.bfloat16)
    columns = columns.reshape(count, FREQ, 2, COLS)
    field = jnp.einsum("pxqk,skqc->spxc", inverse_rows, columns, preferred_element_type=jnp.float32)
    scaled = weights / total_sources
    partial_sum = jnp.sum(scaled[:, None, None, None] * field * field, axis=(0, 1))
    return (field, partial_sum)


def adjoint_spectrum(field, d_int, pupil, weights, tables, total_sources):
    forward_rows, forward_cols, inverse_cols, inverse_rows = tables
    count = pupil.shape[0]
    coeff = 2.0 * weights / total_sources
    d_field = (coeff[:, None, None, None] * d_int[None, None] * field).astype(jnp.bfloat16)
    d_columns = jnp.einsum(
        "pxqk,spxc->skqc", inverse_rows, d_field, preferred_element_type=jnp.float32
    ).astype(jnp.bfloat16)
    d_passed = jnp.dot(
        d_columns.reshape(count * FREQ, 2 * COLS),
        inverse_cols.T,
        preferred_element_type=jnp.float32,
    )
    d_passed = d_passed.reshape(count, FREQ, 2 * FREQ)
    return jnp.sum(d_passed * pupil.astype(jnp.float32), axis=0)


def adjoint_window(d_spectrum, tables):
    forward_rows, forward_cols, inverse_cols, inverse_rows = tables
    d_half = jnp.einsum(
        "kl,pcl->pkc", d_spectrum, forward_cols.astype(jnp.float32), precision=lax.Precision.HIGHEST
    )
    d_half = d_half.reshape(2 * FREQ, COLS)
    return jnp.dot(forward_rows.astype(jnp.float32).T, d_half, precision=lax.Precision.HIGHEST)


def per_device(theta, target, source_shift, source_weight):
    tables = build_tables()
    pupil = pupil_of(source_shift)
    total_sources = SRC_DEV * lax.axis_size("src")
    total_cells = ROWS * lax.axis_size("strip") * COLS
    target_rows = target.astype(jnp.float32)
    resist = jnp.zeros((ROWS, COLS), jnp.float32)
    for iteration in range(ITERS):
        mask_now = jax.nn.sigmoid(theta)
        mask_low = mask_now.astype(jnp.bfloat16)
        window = extended(mask_low, (("strip", 0),), HALO)
        field, partial_sum = imaging(window, pupil, source_weight, tables, total_sources)
        intensity = lax.psum(partial_sum, "src")
        resist = jax.nn.sigmoid(steepness * (intensity - dose_level))
        d_int = 2.0 * (resist - target_rows) * steepness * resist * (1.0 - resist)
        d_spectrum = adjoint_spectrum(field, d_int, pupil, source_weight, tables, total_sources)
        d_window = adjoint_window(lax.psum(d_spectrum, "src"), tables)
        from_next = shifted(d_window[:HALO], "strip", -1)
        from_prev = shifted(d_window[HALO + ROWS :], "strip", 1)
        gradient = d_window[HALO : HALO + ROWS]
        gradient = gradient.at[:HALO].add(from_prev)
        gradient = gradient.at[ROWS - HALO :].add(from_next)
        d_theta = gradient * mask_now * (1.0 - mask_now)
        squares = lax.psum(jnp.sum(d_theta * d_theta), "strip")
        theta = theta - step_size * d_theta * lax.rsqrt(squares / total_cells + epsilon)
    return (theta, resist)


def solution(mesh):
    return jax.shard_map(
        per_device,
        mesh=mesh,
        in_specs=(P(("band", "strip"), None), P(("band", "strip"), None), P("src", None), P("src")),
        out_specs=(P(("band", "strip"), None), P(("band", "strip"), None)),
        check_vma=False,
    )
```

profile of v0, /device:TPU:0, one launch (start us, length us, event | category | flops | bytes accessed | tf_op | source)
XLA Modules:
  0.0 240.5 jit_solution(7867009594235535132)
XLA Ops:
  7.2 0.0 all-reduce.5.cloned.1.call-start
  7.2 1.0 fusion.78
  8.3 3.1 %collective-permute-start = (bf16[64,512]{1,0:T(8,128)(2,1)S(1)}, bf16[64,512]{1,0:T(8,128)(2,1)S(1)}, u32[]{:S(2)}, u32[]{:S(2)}) collective-permute-start(bf16[64,512]{1,0:T(8,128)(2,1)S(1)} %get-tuple-element.60), channel_id=1, source_target_pairs={{0,4},{4,8},{8,12},{12,0},{1,5},{5,9},{9,13},{13,1},{2,6},{6,10},{... | collective-permute-start | bytes 196616 | tf_op jit(solution)/shard_map/ppermute | solution.py:29
  11.3 2.1 collective-permute-start.1
  13.4 1.2 fusion.66
  14.7 1.0 negate_bitcast_fusion
  15.8 0.8 slice_bitcast_fusion.1
  16.5 0.7 broadcast_multiply_fusion.3
  17.2 0.6 fusion.77
  17.8 0.3 negate_convert_fusion.1
  18.1 0.1 add_multiply_fusion.1
  18.2 0.2 fusion.26
  18.5 0.1 fusion.22
  18.6 0.2 convolution_convert_fusion.3
  18.8 0.2 fusion.16
  19.1 2.0 convolution_convert_fusion.1
  21.2 3.3 %reshape.550 = bf16[8,128,2,512]{3,2,1,0:T(2,128)(2,1)S(1)} reshape(bf16[1024,1024]{1,0:T(8,128)(2,1)} %convolution_convert_fusion.1) | data formatting | bytes 4194304 | tf_op jit(solution)/shard_map/reshape | solution.py:93
  24.5 3.0 %fusion = (f32[128,512]{0,1:T(8,128)S(1)}, f32[8,512,2,128,1]{3,1,4,2,0:T(8,128)}) fusion(f32[8]{0:T(128)S(1)} %get-tuple-element.73, bf16[1,128,2,128]{3,1,2,0:T(8,128)(2,1)S(1)} %get-tuple-element.63, bf16[1,128,2,128]{3,1,2,0:T(8,128)(2,1)S(1)} %get-tuple-element.62, bf16[8,128,2,512,1]{3,2,1,0,4:T(2,128)(2,1)S(1)} %bitcast.120), kind=kOutput, calls=%fused_computation.2 | convolution fusion | flops 540213248 | bytes 6684704 | tf_op jit(solution)/shard_map/pxqk,skqc->spxc/dot_general | solution.py:94
  27.5 0.8 copy.21
  28.3 0.0 all-reduce.7.cloned.1.call-start
  28.4 0.2 add_compare_fusion
  28.6 31.5 %all-reduce.5.cloned.1.call-done = f32[128,512]{1,0:T(8,128)} async-done(((f32[128,512]{1,0:T(8,128)}), f32[128,512]{1,0:T(8,128)}) %all-reduce.5.cloned.1.call-update) | async-done | bytes 262160 | tf_op jit(solution)/shard_map/psum | solution.py:138
  60.1 1.1 subtract_multiply_fusion.3
  61.1 0.1 copy.22
  61.3 0.2 broadcast_multiply_fusion.1
  61.5 2.9 %bitcast_convert_fusion.1 = bf16[8,512,2,128]{3,1,2,0:T(8,128)(2,1)S(1)} fusion(f32[8,512,2,128,1]{3,1,4,2,0:T(8,128)} %get-tuple-element.83, f32[8,128,512]{1,2,0:T(8,128)S(1)} %broadcast_multiply_fusion.1, bf16[1,128,2,128]{3,1,2,0:T(8,128)(2,1)S(1)} %get-tuple-element.63, bf16[1,128,2,128]{3,1,2,0:T(8,128)(2,1)S(1)} %get-tuple-element.62), kind=kOutput, calls=%fused_computation.9 | convolution fusion | flops 540082176 | bytes 8519680 | tf_op jit(solution)/shard_map/pxqk,spxc->skqc/dot_general | solution.py:105
  64.5 1.4 fusion.14
  65.9 0.0 all-reduce.9.cloned.1.call-start
  66.0 31.5 %all-reduce.7.cloned.1.call-done = f32[128,256]{1,0:T(8,128)} async-done(((f32[128,256]{1,0:T(8,128)}), f32[128,256]{1,0:T(8,128)}) %all-reduce.7.cloned.1.call-update) | async-done | bytes 131088 | tf_op jit(solution)/shard_map/psum | solution.py:142
  97.5 1.5 fusion.59
  99.0 0.4 fusion.91
  99.5 1.5 collective-permute-start.2
  101.1 2.4 collective-permute-start.3
  103.5 3.5 %collective-permute-done.2 = f32[64,512]{1,0:T(8,128)S(1)} collective-permute-done((f32[64,512]{1,0:T(8,128)S(1)}, f32[64,512]{1,0:T(8,128)S(1)}, u32[]{:S(2)}, u32[]{:S(2)}) %collective-permute-start.2) | collective-permute-done | bytes 131104 | tf_op jit(solution)/shard_map/ppermute | solution.py:40
  107.0 0.8 collective-permute-done.3
  107.9 0.7 multiply_reduce_fusion.1
  108.6 11.6 %psum.44 = f32[]{:T(128)} all-reduce(f32[]{:T(128)} %multiply_reduce_fusion.1), channel_id=1, replica_groups=mesh['band'=2,'strip'=4,'src'=4] {'strip'}, use_global_device_ids=true, to_apply=%region_5.6 | all-reduce | flops 1 | bytes 8 | tf_op jit(solution)/shard_map/psum | solution.py:149
  121.0 0.2 fusion.86
  121.2 0.1 collective-permute-start.4
  121.2 3.8 %collective-permute-start.5 = (bf16[64,512]{1,0:T(8,128)(2,1)S(1)}, bf16[64,512]{1,0:T(8,128)(2,1)S(1)}, u32[]{:S(2)}, u32[]{:S(2)}) collective-permute-start(bf16[64,512]{1,0:T(8,128)(2,1)S(1)} %get-tuple-element.59), channel_id=1, source_target_pairs={{4,0},{8,4},{12,8},{0,12},{5,1},{9,5},{13,9},{1,13},{6,2},{10,6},{... | collective-permute-start | bytes 196616 | tf_op jit(solution)/shard_map/ppermute | solution.py:31
  125.0 2.2 collective-permute-done.4
  127.3 0.2 convolution_convert_fusion.2
  127.5 0.2 fusion.17
  127.8 2.1 convolution_convert_fusion
  129.9 3.3 %reshape.553 = bf16[8,128,2,512]{3,2,1,0:T(2,128)(2,1)S(1)} reshape(bf16[1024,1024]{1,0:T(8,128)(2,1)} %convolution_convert_fusion) | data formatting | bytes 4194304 | tf_op jit(solution)/shard_map/reshape | solution.py:93
  133.2 3.7 %fusion.1 = (f32[128,512]{0,1:T(8,128)}, f32[8,512,2,128,1]{3,1,4,2,0:T(8,128)}) fusion(f32[8]{0:T(128)S(1)} %get-tuple-element.73, bf16[1,128,2,128]{3,1,2,0:T(8,128)(2,1)S(1)} %get-tuple-element.63, bf16[1,128,2,128]{3,1,2,0:T(8,128)(2,1)S(1)} %get-tuple-element.62, bf16[8,128,2,512,1]{3,2,1,0,4:T(2,128)(2,1)S(1)} %bitcast.121), kind=kOutput, calls=%fused_computation.3 | convolution fusion | flops 540213248 | bytes 6684704 | tf_op jit(solution)/shard_map/pxqk,skqc->spxc/dot_general | solution.py:94
  136.9 1.8 copy.26
  138.7 0.0 all-reduce.11.cloned.1.call-start
  138.7 32.7 %all-reduce.9.cloned.1.call-done = f32[128,512]{1,0:T(8,128)} async-done(((f32[128,512]{1,0:T(8,128)}), f32[128,512]{1,0:T(8,128)}) %all-reduce.9.cloned.1.call-update) | async-done | bytes 262160 | tf_op jit(solution)/shard_map/psum | solution.py:138
  171.4 1.8 subtract_multiply_fusion.1
  173.3 0.1 copy.27
  173.4 0.2 broadcast_multiply_fusion
  173.7 3.0 %bitcast_convert_fusion = bf16[8,512,2,128]{3,1,2,0:T(8,128)(2,1)S(1)} fusion(f32[8,512,2,128,1]{3,1,4,2,0:T(8,128)} %get-tuple-element.85, f32[8,128,512]{1,2,0:T(8,128)S(1)} %broadcast_multiply_fusion, bf16[1,128,2,128]{3,1,2,0:T(8,128)(2,1)S(1)} %get-tuple-element.63, bf16[1,128,2,128]{3,1,2,0:T(8,128)(2,1)S(1)} %get-tuple-element.62), kind=kOutput, calls=%fused_computation.8 | convolution fusion | flops 540082176 | bytes 8519680 | tf_op jit(solution)/shard_map/pxqk,spxc->skqc/dot_general | solution.py:105
  176.6 1.4 fusion.15
  178.1 31.6 %all-reduce.11.cloned.1.call-done = f32[128,256]{1,0:T(8,128)} async-done(((f32[128,256]{1,0:T(8,128)}), f32[128,256]{1,0:T(8,128)}) %all-reduce.11.cloned.1.call-update) | async-done | bytes 131088 | tf_op jit(solution)/shard_map/psum | solution.py:142
  209.6 1.5 fusion.57
  211.2 0.4 fusion.92
  211.7 1.5 collective-permute-start.6
  213.2 2.4 collective-permute-start.7
  215.6 3.5 %collective-permute-done.6 = f32[64,512]{1,0:T(8,128)S(1)} collective-permute-done((f32[64,512]{1,0:T(8,128)S(1)}, f32[64,512]{1,0:T(8,128)S(1)}, u32[]{:S(2)}, u32[]{:S(2)}) %collective-permute-start.6) | collective-permute-done | bytes 131104 | tf_op jit(solution)/shard_map/ppermute | solution.py:40
  219.2 0.9 collective-permute-done.7
  220.1 0.8 multiply_reduce_fusion
  220.9 11.5 %psum.47 = f32[]{:T(128)} all-reduce(f32[]{:T(128)} %multiply_reduce_fusion), channel_id=1, replica_groups=mesh['band'=2,'strip'=4,'src'=4] {'strip'}, use_global_device_ids=true, to_apply=%region_11.12 | all-reduce | flops 1 | bytes 8 | tf_op jit(solution)/shard_map/psum | solution.py:149
  233.1 0.9 multiply_subtract_fusion
  (48 shorter events, 0.5 us)
Async XLA Ops:
  7.2 52.9 %all-reduce.5.cloned.1.call-start = ((), (), s32[]{:S(2)}) async-start(), calls=%async_computation | async-start | bytes 524288 | tf_op jit(solution)/shard_map/psum | solution.py:138
  8.3 10.3 %collective-permute-start = (bf16[64,512]{1,0:T(8,128)(2,1)S(1)}, bf16[64,512]{1,0:T(8,128)(2,1)S(1)}, u32[]{:S(2)}, u32[]{:S(2)}) collective-permute-start(bf16[64,512]{1,0:T(8,128)(2,1)S(1)} %get-tuple-element.60), channel_id=1, source_target_pairs={{0,4},{4,8},{8,12},{12,0},{1,5},{5,9},{9,13},{13,1},{2,6},{6,10},{... | collective-permute-start | bytes 196616 | tf_op jit(solution)/shard_map/ppermute | solution.py:29
  11.3 7.2 %collective-permute-start.1 = (bf16[64,512]{1,0:T(8,128)(2,1)S(1)}, bf16[64,512]{1,0:T(8,128)(2,1)S(1)}, u32[]{:S(2)}, u32[]{:S(2)}) collective-permute-start(bf16[64,512]{1,0:T(8,128)(2,1)S(1)} %get-tuple-element.61), channel_id=1, source_target_pairs={{4,0},{8,4},{12,8},{0,12},{5,1},{9,5},{13,9},{1,13},{6,2},{10,6},{... | collective-permute-start | bytes 196616 | tf_op jit(solution)/shard_map/ppermute | solution.py:31
  14.7 4.4 %copy-start.2 = (bf16[128,512]{1,0:T(8,128)(2,1)}, bf16[128,512]{1,0:T(8,128)(2,1)S(1)}, u32[]{:S(2)}) copy-start(bf16[128,512]{1,0:T(8,128)(2,1)S(1)} %get-tuple-element.75) | copy-start | bytes 393220
  14.7 4.4 %copy-start.5 = (bf16[128,512]{1,0:T(8,128)(2,1)}, bf16[128,512]{1,0:T(8,128)(2,1)S(1)}, u32[]{:S(2)}) copy-start(bf16[128,512]{1,0:T(8,128)(2,1)S(1)} %get-tuple-element.76) | copy-start | bytes 393220
  18.4 0.7 copy-start.8
  24.5 35.6 %copy-start.1 = (s32[128,512]{1,0:T(8,128)S(1)}, s32[128,512]{1,0:T(8,128)}, u32[]{:S(2)}) copy-start(s32[128,512]{1,0:T(8,128)} %param.13) | copy-start | bytes 786436
  28.3 69.1 %all-reduce.7.cloned.1.call-start = ((), (), s32[]{:S(2)}) async-start(), calls=%async_computation.1 | async-start | bytes 262144 | tf_op jit(solution)/shard_map/psum | solution.py:142
  28.6 35.8 %copy-start.10 = (pred[8,128,128]{2,1,0:T(32,128)(4,1)}, pred[8,128,128]{2,1,0:T(32,128)(4,1)S(1)}, u32[]{:S(2)}) copy-start(pred[8,128,128]{2,1,0:T(32,128)(4,1)S(1)} %add_compare_fusion) | copy-start | bytes 393220
  61.5 3.0 %copy-start.3 = (bf16[128,512]{1,0:T(8,128)(2,1)S(1)}, bf16[128,512]{1,0:T(8,128)(2,1)}, u32[]{:S(2)}) copy-start(bf16[128,512]{1,0:T(8,128)(2,1)} %copy-done.2) | copy-start | bytes 393220
  61.5 3.0 %copy-start.6 = (bf16[128,512]{1,0:T(8,128)(2,1)S(1)}, bf16[128,512]{1,0:T(8,128)(2,1)}, u32[]{:S(2)}) copy-start(bf16[128,512]{1,0:T(8,128)(2,1)} %copy-done.5) | copy-start | bytes 393220
  65.9 42.0 %copy-start = (f32[128,512]{1,0:T(8,128)S(1)}, f32[128,512]{1,0:T(8,128)}, u32[]{:S(2)}) copy-start(f32[128,512]{1,0:T(8,128)} %param.12) | copy-start | bytes 786436
  65.9 105.5 %all-reduce.9.cloned.1.call-start = ((), (), s32[]{:S(2)}) async-start(), calls=%async_computation.2 | async-start | bytes 524288 | tf_op jit(solution)/shard_map/psum | solution.py:138
  99.5 7.5 %collective-permute-start.2 = (f32[64,512]{1,0:T(8,128)S(1)}, f32[64,512]{1,0:T(8,128)S(1)}, u32[]{:S(2)}, u32[]{:S(2)}) collective-permute-start(f32[64,512]{1,0:T(8,128)S(1)} %get-tuple-element.55), channel_id=1, source_target_pairs={{0,4},{4,8},{8,12},{12,0},{1,5},{5,9},{9,13},{13,1},{2,6},{6,10},{... | collective-permute-start | bytes 393224 | tf_op jit(solution)/shard_map/ppermute | solution.py:40
  101.1 6.8 %collective-permute-start.3 = (f32[64,512]{1,0:T(8,128)S(1)}, f32[64,512]{1,0:T(8,128)S(1)}, u32[]{:S(2)}, u32[]{:S(2)}) collective-permute-start(f32[64,512]{1,0:T(8,128)S(1)} %get-tuple-element.54), channel_id=1, source_target_pairs={{0,12},{4,0},{8,4},{12,8},{1,13},{5,1},{9,5},{13,9},{2,14},{6,2},{... | collective-permute-start | bytes 393224 | tf_op jit(solution)/shard_map/ppermute | solution.py:40
  107.9 19.9 %copy-start.9 = (pred[1024,128]{1,0:T(32,128)(4,1)S(1)}, pred[1024,128]{1,0:T(32,128)(4,1)}, u32[]{:S(2)}) copy-start(pred[1024,128]{1,0:T(32,128)(4,1)} %copy-done.8) | copy-start | bytes 393220
  121.2 6.1 %collective-permute-start.4 = (bf16[64,512]{1,0:T(8,128)(2,1)S(1)}, bf16[64,512]{1,0:T(8,128)(2,1)S(1)}, u32[]{:S(2)}, u32[]{:S(2)}) collective-permute-start(bf16[64,512]{1,0:T(8,128)(2,1)S(1)} %get-tuple-element.58), channel_id=1, source_target_pairs={{0,4},{4,8},{8,12},{12,0},{1,5},{5,9},{9,13},{13,1},{2,6},{6,10},{... | collective-permute-start | bytes 196616 | tf_op jit(solution)/shard_map/ppermute | solution.py:29
  121.2 6.1 %collective-permute-start.5 = (bf16[64,512]{1,0:T(8,128)(2,1)S(1)}, bf16[64,512]{1,0:T(8,128)(2,1)S(1)}, u32[]{:S(2)}, u32[]{:S(2)}) collective-permute-start(bf16[64,512]{1,0:T(8,128)(2,1)S(1)} %get-tuple-element.59), channel_id=1, source_target_pairs={{4,0},{8,4},{12,8},{0,12},{5,1},{9,5},{13,9},{1,13},{6,2},{10,6},{... | collective-permute-start | bytes 196616 | tf_op jit(solution)/shard_map/ppermute | solution.py:31
  138.7 71.0 %all-reduce.11.cloned.1.call-start = ((), (), s32[]{:S(2)}) async-start(), calls=%async_computation.3 | async-start | bytes 262144 | tf_op jit(solution)/shard_map/psum | solution.py:142
  173.6 3.0 %copy-start.4 = (bf16[128,512]{1,0:T(8,128)(2,1)S(1)}, bf16[128,512]{1,0:T(8,128)(2,1)}, u32[]{:S(2)}) copy-start(bf16[128,512]{1,0:T(8,128)(2,1)} %copy-done.2) | copy-start | bytes 393220
  173.6 3.0 %copy-start.7 = (bf16[128,512]{1,0:T(8,128)(2,1)S(1)}, bf16[128,512]{1,0:T(8,128)(2,1)}, u32[]{:S(2)}) copy-start(bf16[128,512]{1,0:T(8,128)(2,1)} %copy-done.5) | copy-start | bytes 393220
  173.6 3.0 %copy-start.11 = (pred[8,128,128]{2,1,0:T(32,128)(4,1)S(1)}, pred[8,128,128]{2,1,0:T(32,128)(4,1)}, u32[]{:S(2)}) copy-start(pred[8,128,128]{2,1,0:T(32,128)(4,1)} %copy-done.10) | copy-start | bytes 393220
  211.7 7.5 %collective-permute-start.6 = (f32[64,512]{1,0:T(8,128)S(1)}, f32[64,512]{1,0:T(8,128)S(1)}, u32[]{:S(2)}, u32[]{:S(2)}) collective-permute-start(f32[64,512]{1,0:T(8,128)S(1)} %get-tuple-element.53), channel_id=1, source_target_pairs={{0,4},{4,8},{8,12},{12,0},{1,5},{5,9},{9,13},{13,1},{2,6},{6,10},{... | collective-permute-start | bytes 393224 | tf_op jit(solution)/shard_map/ppermute | solution.py:40
  213.2 6.8 %collective-permute-start.7 = (f32[64,512]{1,0:T(8,128)S(1)}, f32[64,512]{1,0:T(8,128)S(1)}, u32[]{:S(2)}, u32[]{:S(2)}) collective-permute-start(f32[64,512]{1,0:T(8,128)S(1)} %get-tuple-element.52), channel_id=1, source_target_pairs={{0,12},{4,0},{8,4},{12,8},{1,13},{5,1},{9,5},{13,9},{2,14},{6,2},{... | collective-permute-start | bytes 393224 | tf_op jit(solution)/shard_map/ppermute | solution.py:40
Sparse Core Ops, SparseCore 0:
  28.5 31.5 all-reduce.4
  66.0 31.4 all-reduce.6
  138.8 32.5 all-reduce.8
  178.2 31.4 all-reduce.10
where the time goes:
time: 241 us
  waiting for transfers between devices  138 us (57%)
  matrix products  24.4 us (10%)
  blocking collectives  23.2 us (10%)
  starting transfers between devices  17.1 us (7%)
  between operations  15.6 us (6%)
  other arithmetic  11.5 us (5%)
  local copies, waits for them, and re-layouts  10.5 us (4%)
    psum x2, waiting for transfers between devices, per_device(): intensity = lax.psum(partial_sum, 'src')  64.2 us
    psum x2, waiting for transfers between devices, per_device(): d_window = adjoint_window(lax.psum(d_spectrum, 'src'), tables)  63.1 us
    psum x2, blocking collectives, per_device(): squares = lax.psum(jnp.sum(d_theta * d_theta), 'strip')  23.2 us
    ppermute x4, waiting for transfers between devices, shifted(): lax.ppermute(array, axis, [(i, (i + by) % size) for i in range(size)])  8.78 us
    ppermute x4, starting transfers between devices, shifted(): lax.ppermute(array, axis, [(i, (i + by) % size) for i in range(size)])  7.86 us
    dot_general x2, matrix products, imaging(): jnp.einsum('pxqk,skqc->spxc', inverse_rows, columns, preferred_element_ty...  6.65 us
    reshape x2, local copies, waits for them, and re-layouts, imaging(): columns = columns.reshape(count, FREQ, 2, COLS)  6.61 us
    ppermute x2, starting transfers between devices, extended(): lax.ppermute(head, axis, [((i + 1) % count, i) for i in range(count)])  5.9 us
  transfers between devices with their start and end apart: 12, of which 9 were waited for; matrix products, arithmetic and copies ran while one was open for 2% of the time, Pallas kernels for 0%

commit v1 on v0

--- a/solution.py
+++ b/solution.py
@@ -1,8 +1,13 @@
+import functools
 import math
 
 import jax
 import jax.numpy as jnp
+import ml_dtypes
+import numpy as np
 from jax import lax
+from jax.experimental import pallas as pl
+from jax.experimental.pallas import tpu as pltpu
 from jax.sharding import PartitionSpec as P
 
 ROWS = 128
@@ -151,9 +156,310 @@
     return (theta, resist)
 
 
+MESH = pl.DeviceIdType.MESH
+LANES = 128
+FIRST = FREQ // 2 - 3 * FREQ // 8
+KEPT = FREQ - FIRST
+WIN = ROWS + 2 * HALO
+STEP = 8
+
+
+def host_tables():
+    freq = np.arange(FREQ) - FREQ // 2
+
+    def pair(ids, points, period):
+        angle = 2.0 * np.pi / period * (ids[:, None] % period * points[None, :] % period)
+        return np.cos(angle).astype(np.float32), np.sin(angle).astype(np.float32)
+
+    kept = freq[FIRST:]
+    rc, rs = pair(kept, np.arange(WIN), WIN)
+    rows = np.concatenate([rc, -rs], 0) / WIN
+    cc, cs = pair(freq, np.arange(COLS), COLS)
+    gc = np.concatenate([cc, -cs], 0)
+    gs = np.concatenate([cs, cc], 0)
+    ic, si = pair(kept, np.arange(ROWS) + HALO, WIN)
+    inv = np.block([[ic.T, -si.T], [si.T, ic.T]])
+    return [a.astype(ml_dtypes.bfloat16) for a in (rows, rows.T.copy(), gc, gs, inv, inv.T.copy())]
+
+
+def dot(a, b):
+    return jnp.dot(a, b, preferred_element_type=jnp.float32)
+
+
+def dot_t(a, b):
+    return lax.dot_general(a, b, (((1,), (1,)), ((), ())), preferred_element_type=jnp.float32)
+
+
+def split2(a):
+    high = a.astype(jnp.bfloat16)
+    return high, (a - high.astype(jnp.float32)).astype(jnp.bfloat16)
+
+
+def kernel(
+    n_src, n_strip,
+    shift_ref, weight_ref, theta_ref, target_ref,
+    fr_ref, frt_ref, gc_ref, gs_ref, inv_ref, invt_ref,
+    out_theta, out_resist,
+    thw, mask_own, mask_top, mask_bot, pk, pupil, field, dsp, rs_in, gath, gbuf, res,
+    pk_s, pk_r, halo_s, halo_r, rs_s, rs_r, z_s, z_r, ag_s, ag_r, g_s, g_r, res_s, res_r,
+):
+    me = lax.axis_index("src")
+    strip = lax.axis_index("strip")
+    total = n_src * SRC_DEV
+    src_peers = [lax.rem(me + d, n_src) for d in range(1, n_src)]
+    strip_peers = [lax.rem(strip + d, n_strip) for d in range(1, n_strip)]
+    nxt, prv = strip_peers[0], strip_peers[-1]
+
+    def send(here, there, ssem, rsem, **to):
+        copy = pltpu.make_async_remote_copy(
+            src_ref=here, dst_ref=there, send_sem=ssem, recv_sem=rsem, device_id=to, device_id_type=MESH
+        )
+        copy.start()
+        pending.append(copy)
+        return copy
+
+    pending = []
+    barrier = pltpu.get_barrier_semaphore()
+    for p in src_peers:
+        pl.semaphore_signal(barrier, inc=1, device_id={"src": p}, device_id_type=MESH)
+    for p in strip_peers:
+        pl.semaphore_signal(barrier, inc=1, device_id={"strip": p}, device_id_type=MESH)
+
+    for i in range(SRC_DEV):
+        pk[me, 0, i : i + 1, :] = jnp.full((1, LANES), shift_ref[i, 0].astype(jnp.float32))
+        pk[me, 1, i : i + 1, :] = jnp.full((1, LANES), shift_ref[i, 1].astype(jnp.float32))
+        pk[me, 2, i : i + 1, :] = jnp.full((1, LANES), weight_ref[i] / total)
+    mask_own[...] = jax.nn.sigmoid(theta_ref[...]).astype(jnp.bfloat16)
+    thw[HALO : HALO + ROWS, :] = theta_ref[...]
+    pl.semaphore_wait(barrier, n_src - 1 + n_strip - 1)
+
+    down = send(mask_own.at[ROWS - HALO :], mask_top, halo_s.at[0], halo_r.at[0], strip=nxt)
+    up = send(mask_own.at[:HALO], mask_bot, halo_s.at[1], halo_r.at[1], strip=prv)
+    packs = [send(pk.at[me], pk.at[me], pk_s.at[d], pk_r.at[d], src=p) for d, p in enumerate(src_peers)]
+    th_down = send(theta_ref.at[ROWS - HALO :], thw.at[:HALO], halo_s.at[2], halo_r.at[2], strip=nxt)
+    th_up = send(theta_ref.at[:HALO], thw.at[HALO + ROWS :], halo_s.at[3], halo_r.at[3], strip=prv)
+
+    col = pl.ds(pl.multiple_of(me * LANES, LANES), LANES)
+    g_mine = jnp.concatenate([gc_ref[:, col], gs_ref[:, col]], 1)
+    target_mine = target_ref[:, col].astype(jnp.float32)
+
+    for c in packs:
+        c.wait_recv()
+
+    k_id = lax.broadcasted_iota(jnp.int32, (KEPT, LANES), 0) + (FIRST - FREQ // 2)
+    l_id = lax.broadcasted_iota(jnp.int32, (KEPT, LANES), 1) - FREQ // 2
+    k_id, l_id = k_id.astype(jnp.float32), l_id.astype(jnp.float32)
+    radius = float((FREQ // 4) ** 2)
+
+    def make_pupil(s, carry):
+        q, i = s // SRC_DEV, s % SRC_DEV
+        a = k_id + pk[q, 0, pl.ds(i, 1), :]
+        b = l_id + pk[q, 1, pl.ds(i, 1), :]
+        pupil[s] = jnp.where(a * a + b * b <= radius, 1.0, 0.0).astype(jnp.bfloat16)
+        return carry
+
+    lax.fori_loop(0, total, make_pupil, 0)
+    down.wait_recv()
+    up.wait_recv()
+
+    for it in range(ITERS):
+        last = it == ITERS - 1
+        if it == 0:
+            window = jnp.concatenate([mask_top[...], mask_own[...], mask_bot[...]], 0)
+        else:
+            window = jax.nn.sigmoid(thw[...]).astype(jnp.bfloat16)
+        half = dot(fr_ref[...], window).astype(jnp.bfloat16)
+        spectrum = dot_t(half[:KEPT], gc_ref[...]) + dot_t(half[KEPT:], gs_ref[...])
+        spectrum = (spectrum / COLS).astype(jnp.bfloat16)
+
+        def forward(step, acc):
+            inv = inv_ref[...]
+            for pair in range(STEP // 2):
+                stacked = []
+                for j in range(2):
+                    p = pupil[step * STEP + 2 * pair + j]
+                    passed = spectrum * jnp.concatenate([p, p], 1)
+                    cols = dot(passed, g_mine).astype(jnp.bfloat16)
+                    stacked.append(jnp.concatenate([cols[:, :LANES], cols[:, LANES:]], 0))
+                f = dot(inv, jnp.concatenate(stacked, 1))
+                field[step * (STEP // 2) + pair] = f
+                f2 = f * f
+                for j in range(2):
+                    w = pk[step, 2, 2 * pair + j : 2 * pair + j + 1, :]
+                    part = f2[:, j * LANES : (j + 1) * LANES]
+                    acc = acc + w * (part[:ROWS] + part[ROWS:])
+            return acc
+
+        intensity = lax.fori_loop(0, total // STEP, forward, jnp.zeros((ROWS, LANES), jnp.float32))
+        resist = jax.nn.sigmoid(steepness * (intensity - dose_level))
+        if last:
+            res[me] = resist
+            res_copies = [
+                send(res.at[me], res.at[me], res_s.at[d], res_r.at[d], src=p)
+                for d, p in enumerate(src_peers)
+            ]
+        d_int = 2.0 * (resist - target_mine) * steepness * resist * (1.0 - resist)
+
+        def backward(step, acc):
+            invt = invt_ref[...]
+            for pair in range(STEP // 2):
+                f = field[step * (STEP // 2) + pair]
+                scaled = []
+                for j in range(2):
+                    w = 2.0 * pk[step, 2, 2 * pair + j : 2 * pair + j + 1, :]
+                    d = w * d_int
+                    scaled.append(jnp.concatenate([d, d], 0) * f[:, j * LANES : (j + 1) * LANES])
+                d_field = jnp.concatenate(scaled, 1).astype(jnp.bfloat16)
+                d_cols = dot(invt, d_field).astype(jnp.bfloat16)
+                for j in range(2):
+                    mine = d_cols[:, j * LANES : (j + 1) * LANES]
+                    flat = jnp.concatenate([mine[:KEPT], mine[KEPT:]], 1)
+                    p = pupil[step * STEP + 2 * pair + j].astype(jnp.float32)
+                    acc = acc + jnp.concatenate([p, p], 1) * dot_t(flat, g_mine)
+            return acc
+
+        d_spec = lax.fori_loop(0, total // STEP, backward, jnp.zeros((KEPT, 2 * LANES), jnp.float32))
+        part = KEPT // 2
+        for q in range(n_src):
+            r, c = q // 2, q % 2
+            dsp[it, q] = d_spec[r * part : (r + 1) * part, c * LANES : (c + 1) * LANES]
+        scatter = [
+            send(dsp.at[it, p], rs_in.at[it, d], rs_s.at[it, d], rs_r.at[it, d], src=p)
+            for d, p in enumerate(src_peers)
+        ]
+        mine = dsp[it, me]
+        for d, c in enumerate(scatter):
+            c.wait_recv()
+            mine = mine + rs_in[it, d]
+        gath[it, 0, me] = mine
+        z_next = send(gath.at[it, 0, me], gath.at[it, 1, me], z_s.at[it, 0], z_r.at[it, 0], strip=nxt)
+        z_prev = send(gath.at[it, 0, me], gath.at[it, 2, me], z_s.at[it, 1], z_r.at[it, 1], strip=prv)
+
+        def share(rel):
+            return [
+                send(gath.at[it, rel, me], gath.at[it, rel, me], ag_s.at[it, rel, d], ag_r.at[it, rel, d], src=p)
+                for d, p in enumerate(src_peers)
+            ]
+
+        shares = share(0)
+        z_next.wait_recv()
+        shares = shares + share(1)
+        z_prev.wait_recv()
+        shares = shares + share(2)
+
+        def d_half(rel):
+            full = jnp.concatenate(
+                [jnp.concatenate([gath[it, rel, 0], gath[it, rel, 1]], 1),
+                 jnp.concatenate([gath[it, rel, 2], gath[it, rel, 3]], 1)], 0)
+            high, low = split2(full / COLS)
+            both = jnp.concatenate([high, low], 0)
+            out = []
+            for g in (gc_ref, gs_ref):
+                o = dot(both, g[...])
+                out.append(o[:KEPT] + o[KEPT:])
+            return split2(jnp.concatenate(out, 0))
+
+        def back_rows(lo, hi, parts):
+            t = frt_ref[lo:hi, :]
+            return dot(t, parts[0]) + dot(t, parts[1])
+
+        for c in shares[: n_src - 1]:
+            c.wait_recv()
+        own = d_half(0)
+        center = back_rows(HALO, HALO + ROWS, own) if last else back_rows(0, WIN, own)
+        for c in shares[n_src - 1 : 2 * (n_src - 1)]:
+            c.wait_recv()
+        prev = d_half(1)
+        top = back_rows(HALO + ROWS if last else ROWS, WIN, prev)
+        for c in shares[2 * (n_src - 1) :]:
+            c.wait_recv()
+        after = d_half(2)
+        bottom = back_rows(0, HALO if last else WIN - ROWS, after)
+        gradient = center + jnp.concatenate([top, bottom], 0)
+        if it == 0:
+            th_down.wait_recv()
+            th_up.wait_recv()
+        theta_now = thw[HALO : HALO + ROWS, :] if last else thw[...]
+        m = jax.nn.sigmoid(theta_now)
+        d_theta = gradient * m * (1.0 - m)
+        inner = d_theta if last else d_theta[HALO : HALO + ROWS]
+        sq = inner * inner
+        sq = jnp.sum(sq.reshape(ROWS // 8, 8, COLS), axis=0)
+        tile = sq[:, :LANES]
+        for c in range(1, COLS // LANES):
+            tile = tile + sq[:, c * LANES : (c + 1) * LANES]
+        gbuf[it, strip] = tile
+        norms = [
+            send(gbuf.at[it, strip], gbuf.at[it, strip], g_s.at[it, d], g_r.at[it, d], strip=p)
+            for d, p in enumerate(strip_peers)
+        ]
+        for c in norms:
+            c.wait_recv()
+        squares = jnp.sum(gbuf[it], axis=0)
+        squares = jnp.sum(jnp.sum(squares, axis=1, keepdims=True), axis=0, keepdims=True)
+        scale = step_size * lax.rsqrt(squares / (ROWS * n_strip * COLS) + epsilon)
+        theta_new = theta_now - d_theta * scale
+        if last:
+            out_theta[...] = theta_new
+            for c in res_copies:
+                c.wait_recv()
+            for q in range(n_src):
+                out_resist[:, q * LANES : (q + 1) * LANES] = res[q]
+        else:
+            thw[...] = theta_new
+    for c in pending:
+        c.wait_send()
+
+
+def per_device_fused(n_src, n_strip, theta, target, source_shift, source_weight):
+    tables = [jnp.asarray(t) for t in host_tables()]
+    total = n_src * SRC_DEV
+    part = KEPT // 2
+    vm = pl.BlockSpec(memory_space=pltpu.VMEM)
+    sm = pl.BlockSpec(memory_space=pltpu.SMEM)
+    f32, bf16, dma = jnp.float32, jnp.bfloat16, pltpu.SemaphoreType.DMA
+    shape = jax.ShapeDtypeStruct((ROWS, COLS), f32)
+    ns, nz = n_src - 1, n_strip - 1
+    return pl.pallas_call(
+        functools.partial(kernel, n_src, n_strip),
+        out_shape=(shape, shape),
+        in_specs=[sm, sm] + [vm] * 8,
+        out_specs=(vm, vm),
+        scratch_shapes=[
+            pltpu.VMEM((WIN, COLS), f32),
+            pltpu.VMEM((ROWS, COLS), bf16),
+            pltpu.VMEM((HALO, COLS), bf16),
+            pltpu.VMEM((HALO, COLS), bf16),
+            pltpu.VMEM((n_src, 3, SRC_DEV, LANES), f32),
+            pltpu.VMEM((total, KEPT, LANES), bf16),
+            pltpu.VMEM((total // 2, 2 * ROWS, 2 * LANES), f32),
+            pltpu.VMEM((ITERS, n_src, part, LANES), f32),
+            pltpu.VMEM((ITERS, ns, part, LANES), f32),
+            pltpu.VMEM((ITERS, 3, n_src, part, LANES), f32),
+            pltpu.VMEM((ITERS, n_strip, 8, LANES), f32),
+            pltpu.VMEM((n_src, ROWS, LANES), f32),
+            dma((ns,)), dma((ns,)),
+            dma((4,)), dma((4,)),
+            dma((ITERS, ns)), dma((ITERS, ns)),
+            dma((ITERS, 2)), dma((ITERS, 2)),
+            dma((ITERS, 3, ns)), dma((ITERS, 3, ns)),
+            dma((ITERS, nz)), dma((ITERS, nz)),
+            dma((ns,)), dma((ns,)),
+        ],
+        compiler_params=pltpu.CompilerParams(
+            collective_id=0, has_side_effects=True, vmem_limit_bytes=48 * 1024 * 1024
+        ),
+    )(source_shift, source_weight, theta, target, *tables)
+
+
 def solution(mesh):
+    n_src, n_strip = mesh.shape["src"], mesh.shape["strip"]
+    if n_src * LANES == COLS and n_strip > 2:
+        body = functools.partial(per_device_fused, n_src, n_strip)
+    else:
+        body = per_device
     return jax.shard_map(
-        per_device,
+        body,
         mesh=mesh,
         in_specs=(P(("band", "strip"), None), P(("band", "strip"), None), P("src", None), P("src")),
         out_specs=(P(("band", "strip"), None), P(("band", "strip"), None)),

time: 241 us -> 64.7 us (0.27)
  waiting for transfers between devices: 138 us -> 0 us
  Pallas kernels: 0 us -> 54.1 us
  matrix products: 24.4 us -> 0 us
  blocking collectives: 23.2 us -> 0 us
  starting transfers between devices: 17.1 us -> 0 us
  between operations: 15.6 us -> 0.66 us
  other arithmetic: 11.5 us -> 0 us
    psum x4 -> x0, waiting for transfers between devices: 127 us -> none  [the longest x2 64.2 us: per_device(): intensity = lax.psum(partial_sum, 'src')]
    pallas_call x0 -> x1, Pallas kernels: none -> 54.1 us  [per_device_fused(): pl.pallas_call(functools.partial(kernel, n_src, n_strip), out_shape=(shap...]
    dot_general x16 -> x0, matrix products: 24.4 us -> none  [the longest x2 6.65 us: imaging(): jnp.einsum('pxqk,skqc->spxc', inverse_rows, columns, preferred_element_ty...]
    psum x2 -> x0, blocking collectives: 23.2 us -> none  [per_device(): squares = lax.psum(jnp.sum(d_theta * d_theta), 'strip')]
    ppermute x8 -> x0, starting transfers between devices: 16.9 us -> none  [the longest x4 7.86 us: shifted(): lax.ppermute(array, axis, [(i, (i + by) % size) for i in range(size)])]
    ppermute x8 -> x0, waiting for transfers between devices: 11 us -> none  [the longest x4 8.78 us: shifted(): lax.ppermute(array, axis, [(i, (i + by) % size) for i in range(size)])]
    unnamed x24 -> x21, local copies, waits for them, and re-layouts: 0.06 us -> 9.57 us
    reshape x2 -> x0, local copies, waits for them, and re-layouts: 6.61 us -> none  [imaging(): columns = columns.reshape(count, FREQ, 2, COLS)]
  transfers between devices with their start and end apart: 12 -> 0, of which waited for: 9 -> 0; matrix products, arithmetic and copies ran while one was open for 2% -> 0% of each run, Pallas kernels for 0% -> 0%
where the time goes in v1:
time: 64.7 us; the launch traced here: 64.3 us
  Pallas kernels  54.1 us (84%)
  local copies, waits for them, and re-layouts  9.57 us (15%)
  between operations  0.66 us (1%)
    pallas_call x1, Pallas kernels, per_device_fused(): pl.pallas_call(functools.partial(kernel, n_src, n_strip), out_shape=(shap...  54.1 us
    unnamed x21, local copies, waits for them, and re-layouts  9.57 us

profile of v1, /device:TPU:0, one launch (start us, length us, event | category | flops | bytes accessed | tf_op | source)
XLA Modules:
  0.0 64.3 jit_solution(9448239543099612454)
XLA Ops:
  0.6 0.0 copy-start.8
  0.6 0.8 %copy.12.shift_ref = s32[8,2]{1,0:T(8,128)S(1)} copy(s32[8,2]{0,1:T(2,128)} %param.12) | data formatting | bytes 128 | tf_op args[2]
  1.4 0.0 copy-done.8
  1.4 0.0 copy-start
  1.4 0.9 %copy-done = f32[128,512]{1,0:T(8,128)S(1)} copy-done((f32[128,512]{1,0:T(8,128)S(1)}, f32[128,512]{1,0:T(8,128)}, u32[]{:S(2)}) %copy-start) | copy-done | bytes 262168
  2.4 0.0 copy-start.1
  2.4 0.9 %copy-done.1 = s32[128,512]{1,0:T(8,128)S(1)} copy-done((s32[128,512]{1,0:T(8,128)S(1)}, s32[128,512]{1,0:T(8,128)}, u32[]{:S(2)}) %copy-start.1) | copy-done | bytes 262168
  3.3 0.0 copy-start.2
  3.3 0.9 %copy-done.2 = bf16[256,512]{1,0:T(8,128)(2,1)S(1)} copy-done((bf16[256,512]{1,0:T(8,128)(2,1)S(1)}, bf16[256,512]{1,0:T(8,128)(2,1)}, u32[]{:S(2)}) %copy-start.2) | copy-done | bytes 262168
  4.3 0.0 copy-start.3
  4.3 0.9 %copy-done.3 = bf16[256,512]{1,0:T(8,128)(2,1)S(1)} copy-done((bf16[256,512]{1,0:T(8,128)(2,1)S(1)}, bf16[256,512]{1,0:T(8,128)(2,1)}, u32[]{:S(2)}) %copy-start.3) | copy-done | bytes 262168
  5.2 0.0 copy-start.4
  5.2 0.9 %copy-done.4 = bf16[256,224]{1,0:T(8,128)(2,1)S(1)} copy-done((bf16[256,224]{1,0:T(8,128)(2,1)S(1)}, bf16[256,224]{1,0:T(8,128)(2,1)}, u32[]{:S(2)}) %copy-start.4) | copy-done | bytes 114712
  6.1 0.0 copy-start.5
  6.1 0.9 %copy-done.5 = bf16[256,224]{1,0:T(8,128)(2,1)S(1)} copy-done((bf16[256,224]{1,0:T(8,128)(2,1)S(1)}, bf16[256,224]{1,0:T(8,128)(2,1)}, u32[]{:S(2)}) %copy-start.5) | copy-done | bytes 114712
  7.0 0.0 copy-start.6
  7.0 0.9 %copy-done.6 = bf16[224,256]{1,0:T(8,128)(2,1)S(1)} copy-done((bf16[224,256]{1,0:T(8,128)(2,1)S(1)}, bf16[224,256]{1,0:T(8,128)(2,1)}, u32[]{:S(2)}) %copy-start.6) | copy-done | bytes 114712
  7.9 0.0 copy-start.7
  7.9 0.9 %copy-done.7 = bf16[224,256]{1,0:T(8,128)(2,1)S(1)} copy-done((bf16[224,256]{1,0:T(8,128)(2,1)S(1)}, bf16[224,256]{1,0:T(8,128)(2,1)}, u32[]{:S(2)}) %copy-start.7) | copy-done | bytes 114712
  8.8 54.1 %shard_map.113 = (f32[128,512]{1,0:T(8,128)S(1)}, f32[128,512]{1,0:T(8,128)S(1)}) custom-call(s32[8,2]{1,0:T(8,128)S(1)} %copy.12.shift_ref, f32[8]{0:T(128)S(1)} %copy-done.8, f32[128,512]{1,0:T(8,128)S(1)} %copy-done, s32[128,512]{1,0:T(8,128)S(1)} %copy-done.1, bf16[224,256]{1,0:T(8,128)(2,1)S(1)} %copy-done.7, bf16[256,224]{1,0:T(8,128)(2,1)S(1)} %copy-done.5, ...), custom_call_target="tpu_custom_call" | custom-call | tf_op jit(solution)/shard_map/pallas_call | solution.py:423
  62.9 0.7 %copy.15 = f32[128,512]{1,0:T(8,128)} copy(f32[128,512]{1,0:T(8,128)S(1)} %get-tuple-element.4) | data formatting | bytes 524288
  63.6 0.7 %copy.16 = f32[128,512]{1,0:T(8,128)} copy(f32[128,512]{1,0:T(8,128)S(1)} %get-tuple-element.5) | data formatting | bytes 524288
Async XLA Ops:
  0.6 0.8 %copy-start.8 = (f32[8]{0:T(128)S(1)}, f32[8]{0:T(128)}, u32[]{:S(2)}) copy-start(f32[8]{0:T(128)} %weight_ref.1) | copy-start | bytes 100
  1.4 1.0 %copy-start = (f32[128,512]{1,0:T(8,128)S(1)}, f32[128,512]{1,0:T(8,128)}, u32[]{:S(2)}) copy-start(f32[128,512]{1,0:T(8,128)} %theta_ref.1) | copy-start | bytes 786436
  2.4 0.9 %copy-start.1 = (s32[128,512]{1,0:T(8,128)S(1)}, s32[128,512]{1,0:T(8,128)}, u32[]{:S(2)}) copy-start(s32[128,512]{1,0:T(8,128)} %target_ref.1) | copy-start | bytes 786436
  3.3 0.9 %copy-start.2 = (bf16[256,512]{1,0:T(8,128)(2,1)S(1)}, bf16[256,512]{1,0:T(8,128)(2,1)}, u32[]{:S(2)}) copy-start(bf16[256,512]{1,0:T(8,128)(2,1)} %constant.15.clone.gs_ref) | copy-start | bytes 786436
  4.3 0.9 %copy-start.3 = (bf16[256,512]{1,0:T(8,128)(2,1)S(1)}, bf16[256,512]{1,0:T(8,128)(2,1)}, u32[]{:S(2)}) copy-start(bf16[256,512]{1,0:T(8,128)(2,1)} %constant.14.clone.gc_ref) | copy-start | bytes 786436
  5.2 0.9 %copy-start.4 = (bf16[256,224]{1,0:T(8,128)(2,1)S(1)}, bf16[256,224]{1,0:T(8,128)(2,1)}, u32[]{:S(2)}) copy-start(bf16[256,224]{1,0:T(8,128)(2,1)} %constant.16.clone.inv_ref) | copy-start | bytes 344068
  6.1 0.9 %copy-start.5 = (bf16[256,224]{1,0:T(8,128)(2,1)S(1)}, bf16[256,224]{1,0:T(8,128)(2,1)}, u32[]{:S(2)}) copy-start(bf16[256,224]{1,0:T(8,128)(2,1)} %constant.13.clone.frt_ref) | copy-start | bytes 344068
  7.0 0.9 %copy-start.6 = (bf16[224,256]{1,0:T(8,128)(2,1)S(1)}, bf16[224,256]{1,0:T(8,128)(2,1)}, u32[]{:S(2)}) copy-start(bf16[224,256]{1,0:T(8,128)(2,1)} %constant.17.clone.invt_ref) | copy-start | bytes 344068
  7.9 0.9 %copy-start.7 = (bf16[224,256]{1,0:T(8,128)(2,1)S(1)}, bf16[224,256]{1,0:T(8,128)(2,1)}, u32[]{:S(2)}) copy-start(bf16[224,256]{1,0:T(8,128)(2,1)} %constant.12.clone.fr_ref) | copy-start | bytes 344068

commit v2 on v1

--- a/solution.py
+++ b/solution.py
@@ -197,11 +197,12 @@
 
 def kernel(
     n_src, n_strip,
-    shift_ref, weight_ref, theta_ref, target_ref,
-    fr_ref, frt_ref, gc_ref, gs_ref, inv_ref, invt_ref,
+    shift_ref, weight_ref, theta_hbm, target_hbm,
+    fr_hbm, frt_hbm, gc_hbm, gs_hbm, inv_hbm, invt_hbm,
     out_theta, out_resist,
     thw, mask_own, mask_top, mask_bot, pk, pupil, field, dsp, rs_in, gath, gbuf, res,
     pk_s, pk_r, halo_s, halo_r, rs_s, rs_r, z_s, z_r, ag_s, ag_r, g_s, g_r, res_s, res_r,
+    theta_ref, target_ref, fr_ref, frt_ref, gc_ref, gs_ref, inv_ref, invt_ref, in_s,
 ):
     me = lax.axis_index("src")
     strip = lax.axis_index("strip")
@@ -218,7 +219,18 @@
         pending.append(copy)
         return copy
 
-    pending = []
+    def fetch(here, there):
+        copy = pltpu.make_async_copy(here, there, in_s.at[len(fetches)])
+        copy.start()
+        fetches.append(copy)
+        return copy
+
+    pending, fetches = [], []
+    theta_in = fetch(theta_hbm, theta_ref)
+    fr_in = fetch(fr_hbm, fr_ref)
+    gc_in, gs_in = fetch(gc_hbm, gc_ref), fetch(gs_hbm, gs_ref)
+    inv_in, target_in = fetch(inv_hbm, inv_ref), fetch(target_hbm, target_ref)
+    invt_in, frt_in = fetch(invt_hbm, invt_ref), fetch(frt_hbm, frt_ref)
     barrier = pltpu.get_barrier_semaphore()
     for p in src_peers:
         pl.semaphore_signal(barrier, inc=1, device_id={"src": p}, device_id_type=MESH)
@@ -226,9 +238,10 @@
         pl.semaphore_signal(barrier, inc=1, device_id={"strip": p}, device_id_type=MESH)
 
     for i in range(SRC_DEV):
-        pk[me, 0, i : i + 1, :] = jnp.full((1, LANES), shift_ref[i, 0].astype(jnp.float32))
-        pk[me, 1, i : i + 1, :] = jnp.full((1, LANES), shift_ref[i, 1].astype(jnp.float32))
+        pk[me, 0, i : i + 1, :] = jnp.full((1, LANES), shift_ref[0, i].astype(jnp.float32))
+        pk[me, 1, i : i + 1, :] = jnp.full((1, LANES), shift_ref[1, i].astype(jnp.float32))
         pk[me, 2, i : i + 1, :] = jnp.full((1, LANES), weight_ref[i] / total)
+    theta_in.wait()
     mask_own[...] = jax.nn.sigmoid(theta_ref[...]).astype(jnp.bfloat16)
     thw[HALO : HALO + ROWS, :] = theta_ref[...]
     pl.semaphore_wait(barrier, n_src - 1 + n_strip - 1)
@@ -240,6 +253,8 @@
     th_up = send(theta_ref.at[:HALO], thw.at[HALO + ROWS :], halo_s.at[3], halo_r.at[3], strip=prv)
 
     col = pl.ds(pl.multiple_of(me * LANES, LANES), LANES)
+    for c in fetches[1:]:
+        c.wait()
     g_mine = jnp.concatenate([gc_ref[:, col], gs_ref[:, col]], 1)
     target_mine = target_ref[:, col].astype(jnp.float32)
 
@@ -416,6 +431,7 @@
     total = n_src * SRC_DEV
     part = KEPT // 2
     vm = pl.BlockSpec(memory_space=pltpu.VMEM)
+    hbm = pl.BlockSpec(memory_space=pltpu.HBM)
     sm = pl.BlockSpec(memory_space=pltpu.SMEM)
     f32, bf16, dma = jnp.float32, jnp.bfloat16, pltpu.SemaphoreType.DMA
     shape = jax.ShapeDtypeStruct((ROWS, COLS), f32)
@@ -423,7 +439,7 @@
     return pl.pallas_call(
         functools.partial(kernel, n_src, n_strip),
         out_shape=(shape, shape),
-        in_specs=[sm, sm] + [vm] * 8,
+        in_specs=[sm, sm] + [hbm] * 8,
         out_specs=(vm, vm),
         scratch_shapes=[
             pltpu.VMEM((WIN, COLS), f32),
@@ -445,11 +461,15 @@
             dma((ITERS, 3, ns)), dma((ITERS, 3, ns)),
             dma((ITERS, nz)), dma((ITERS, nz)),
             dma((ns,)), dma((ns,)),
+            pltpu.VMEM((ROWS, COLS), f32),
+            pltpu.VMEM((ROWS, COLS), jnp.int32),
+            *[pltpu.VMEM(t.shape, bf16) for t in tables],
+            dma((8,)),
         ],
         compiler_params=pltpu.CompilerParams(
-            collective_id=0, has_side_effects=True, vmem_limit_bytes=48 * 1024 * 1024
+            collective_id=0, has_side_effects=True, vmem_limit_bytes=64 * 1024 * 1024
         ),
-    )(source_shift, source_weight, theta, target, *tables)
+    )(source_shift.T, source_weight, theta, target, *tables)
 
 
 def solution(mesh):

time: 64.7 us -> 58.4 us (0.903)
  local copies, waits for them, and re-layouts: 9.57 us -> 2.42 us
  Pallas kernels: 54.1 us -> 55 us
    unnamed x21 -> x4, local copies, waits for them, and re-layouts: 9.57 us -> 2.42 us
    pallas_call x1, Pallas kernels: 54.1 us -> 55 us  [per_device_fused(): pl.pallas_call(functools.partial(kernel, n_src, n_strip), out_shape=(shap...]
where the time goes in v2:
time: 58.4 us; the launch traced here: 58.1 us
  Pallas kernels  55 us (94%)
  local copies, waits for them, and re-layouts  2.42 us (4%)
  between operations  0.65 us (1%)
    pallas_call x1, Pallas kernels, per_device_fused(): pl.pallas_call(functools.partial(kernel, n_src, n_strip), out_shape=(shap...  55 us
    unnamed x4, local copies, waits for them, and re-layouts  2.42 us

profile of v2, /device:TPU:0, one launch (start us, length us, event | category | flops | bytes accessed | tf_op | source)
XLA Modules:
  0.0 58.1 jit_solution(10494848606665754718)
XLA Ops:
  0.6 55.0 %shard_map.113 = (f32[128,512]{1,0:T(8,128)}, f32[128,512]{1,0:T(8,128)}) custom-call(s32[2,8]{1,0:T(2,128)} %bitcast.1, f32[8]{0:T(128)} %weight_ref.1, f32[128,512]{1,0:T(8,128)} %theta_hbm.1, s32[128,512]{1,0:T(8,128)} %target_hbm.1, bf16[224,256]{1,0:T(8,128)(2,1)} %constant.12.clone.fr_hbm, bf16[256,224]{1,0:T(8,128)(2,1)} %constant.13.clone.frt_hbm, ...), custom_call_target="tpu_custom_call" | custom-call | tf_op jit(solution)/shard_map/pallas_call | solution.py:439
  55.7 0.0 copy-start
  55.7 1.7 %copy.14 = f32[128,512]{1,0:T(8,128)} copy(f32[128,512]{1,0:T(8,128)} %get-tuple-element.4) | data formatting | bytes 524288
  57.4 0.0 copy-done
  57.4 0.7 %copy.15 = f32[128,512]{1,0:T(8,128)} copy(f32[128,512]{1,0:T(8,128)S(1)} %copy-done) | data formatting | bytes 524288
Async XLA Ops:
  55.7 1.7 %copy-start = (f32[128,512]{1,0:T(8,128)S(1)}, f32[128,512]{1,0:T(8,128)}, u32[]{:S(2)}) copy-start(f32[128,512]{1,0:T(8,128)} %get-tuple-element.5) | copy-start | bytes 786436
